TPU v7x, 32 devices: a whole 2x2x4 slice. The times are simulated.
32 devices in a mesh: sub: 8 (over z, y), coarse: 4 (over x, core).
Axes of the slice: x: 2, y: 2, z: 4, core: 2. Of those that a mesh axis runs over, the one named last changes fastest.
Arguments:
- right_side: float32 [8, 24576], P(None, 'sub'), may hold values from -6 to 6
- dual_ops: bfloat16 [32, 1536, 1536], P('sub', 'coarse'), may hold values from -8 to 72, as said below
- precond_ops: bfloat16 [32, 1536, 1536], P('sub', 'coarse'), may hold values from -8 to 72, as said below
- corner_ops: bfloat16 [32, 24, 1536], P('sub'), may hold values from -0.15625 to 0.15625
- coarse_inverse: float32 [64, 64], P('coarse'), may hold values from -8 to 72, as said below
- sub_index: int32 [32, 1536], P('sub'), may hold values from 0 to 24575, as said below
- corner_map: int32 [32, 24], P('sub'), may hold values from 0 to 63
Outputs:
- multipliers: float32 [8, 24576], P(None, 'sub')
- residual: float32 [8, 24576], P(None, 'sub')
Inputs may be any that keep to these rules, and one draw needn't show every extreme that they name: `sub_index`: every multiplier number stands in exactly two slots in all: one in the first half of some subdomain's slots and one in the second half of some subdomain's slots. With multiplier i owned by index i // 3072 of sub and subdomain s by index s // 4, a subdomain's first-half slots hold only multipliers of its own index, its second-half slots only multipliers of its own index or of the index before it (cyclically), and half of every index's multipliers have their second slot on the next index. `dual_ops`: symmetric positive definite. `precond_ops`: symmetric positive definite. `coarse_inverse`: symmetric positive definite.
All inputs are finite; a program needn't handle non-finite values.
Results may differ from a plain program's by a relative error of at most 0.022.
Values may be sent and summed in bfloat16 or wider, within the bound.
A program may use at most 128 MiB of HBM per device.

v0:
```python
import jax
import jax.numpy as jnp
from jax import lax
from jax.sharding import PartitionSpec as P

ITERS = 4


HIGH = lax.Precision.HIGHEST


def passed_along(value, axis, steps):
    count = lax.axis_size(axis)
    pairs = [(source, (source + steps) % count) for source in range(count)]
    return lax.ppermute(value, axis, pairs)


def per_device(
    right_side, dual_ops, precond_ops, corner_ops, coarse_inverse, sub_index, corner_map
):
    cases, lam_rows = right_side.shape
    subs, block_rows, order = dual_ops.shape
    coarse_dofs = coarse_inverse.shape[1]
    here = lax.axis_index("sub")
    mine = lax.axis_index("coarse")
    total_rows = lam_rows * lax.axis_size("sub")
    local_pos = jnp.mod(sub_index - (here - 1) * lam_rows, total_rows)
    signs = jnp.where(jnp.arange(order) < order // 2, 1.0, -1.0).astype(jnp.float32)
    row_start = mine * block_rows
    block_pos = lax.dynamic_slice_in_dim(local_pos, row_start, block_rows, 1)
    block_signs = lax.dynamic_slice_in_dim(signs, row_start, block_rows, 0)
    block_corner = lax.dynamic_slice_in_dim(corner_ops, row_start, block_rows, 2)
    corner_table = (corner_map.reshape(-1)[:, None] == jnp.arange(coarse_dofs)[None, :]).astype(
        jnp.float32
    )

    def coarse_answer(gathered):
        lifted = jnp.einsum(
            "scn,ksn->ksc", corner_ops, gathered, preferred_element_type=jnp.float32
        )
        partial_load = jnp.dot(lifted.reshape(cases, -1), corner_table, precision=HIGH)
        load = lax.psum(partial_load, "sub")
        own_part = jnp.dot(load, coarse_inverse.T, precision=HIGH).astype(jnp.bfloat16)
        answer = lax.all_gather(own_part, "coarse", axis=1, tiled=True)
        return answer[:, corner_map]

    def apply_operator(vectors, matrices, with_coarse):
        previous = passed_along(vectors.astype(jnp.bfloat16), "sub", 1).astype(vectors.dtype)
        window = jnp.concatenate([previous, vectors], axis=1)
        gathered = (window[:, local_pos] * signs).astype(jnp.bfloat16)
        spread_back = coarse_answer(gathered) if with_coarse else None
        products = jnp.einsum(
            "smn,ksn->ksm", matrices, gathered, preferred_element_type=jnp.float32
        )
        terms = products
        if with_coarse:
            terms = terms + jnp.einsum(
                "scm,ksc->ksm", block_corner, spread_back, preferred_element_type=jnp.float32
            )
        terms = terms * block_signs
        sums = (
            jnp.zeros((cases, lam_rows + lam_rows), jnp.float32)
            .at[:, block_pos.reshape(-1)]
            .add(terms.reshape(cases, -1))
        )
        sums = lax.psum(sums, "coarse")
        returned = passed_along(sums[:, :lam_rows], "sub", -1)
        return sums[:, lam_rows:] + returned

    def fit_of(residual, pre):
        return lax.psum(jnp.sum(residual * pre, axis=1), "sub")

    multipliers = jnp.zeros_like(right_side)
    residual = right_side
    pre = apply_operator(residual, precond_ops, False)
    fit = fit_of(residual, pre)
    direction = pre
    for step in range(ITERS):
        image = apply_operator(direction, dual_ops, True)
        alpha = fit / lax.psum(jnp.sum(direction * image, axis=1), "sub")
        multipliers = multipliers + alpha[:, None] * direction
        residual = residual - alpha[:, None] * image
        if step + 1 < ITERS:
            pre = apply_operator(residual, precond_ops, False)
            fit_next = fit_of(residual, pre)
            direction = pre + (fit_next / fit)[:, None] * direction
            fit = fit_next
    return (multipliers, residual)


def solution(mesh):
    placed = (
        P(None, "sub"),
        P("sub", "coarse", None),
        P("sub", "coarse", None),
        P("sub", None, None),
        P("coarse", None),
        P("sub", None),
        P("sub", None),
    )
    return jax.shard_map(
        per_device,
        mesh=mesh,
        in_specs=placed,
        out_specs=(P(None, "sub"), P(None, "sub")),
        check_vma=False,
    )
```

profile of v0, /device:TPU:0, one launch (start us, length us, event | category | flops | bytes accessed | tf_op | source)
XLA Modules:
  0.0 989.6 jit_solution(13428400682340185514)
XLA Ops:
  19.7 20.9 %gather_fusion = f32[6144,8]{1,0:T(8,128)} fusion(f32[8,6144]{0,1:T(8,128)S(1)} %copy.198, s32[6144]{0:T(1024)S(1)} %broadcast_clamp_fusion), kind=kCustom, calls=%fused_computation | custom fusion | bytes 417792 | tf_op jit(solution)/shard_map/gather | solution.py:50
  47.7 9.9 scatter_custom_fusion
  59.4 30.5 %all-reduce.10.cloned.1.call-done = f32[8,6144]{1,0:T(8,128)} async-done(((f32[8,6144]{1,0:T(8,128)}), f32[8,6144]{1,0:T(8,128)}) %all-reduce.10.cloned.1.call-update) | async-done | bytes 196624 | tf_op jit(solution)/shard_map/psum | solution.py:66
  108.0 22.9 %gather_fusion.1 = f32[6144,8]{1,0:T(8,128)} fusion(f32[8,6144]{0,1:T(8,128)S(1)} %copy.202, s32[6144]{0:T(1024)} %copy-done.3), kind=kCustom, calls=%fused_computation.1 | custom fusion | bytes 417792 | tf_op jit(solution)/shard_map/gather | solution.py:50
  137.4 19.1 %psum.142 = f32[8,64]{1,0:T(8,128)S(1)} all-reduce(f32[8,64]{1,0:T(8,128)S(1)} %fusion.43), channel_id=1, replica_groups=mesh['sub'=8,'coarse'=4] {'sub'}, use_global_device_ids=true, to_apply=%region_4.5 | all-reduce | flops 512 | bytes 4096 | tf_op jit(solution)/shard_map/psum | solution.py:42
  163.9 9.9 scatter_custom_fusion.1
  175.7 28.1 %all-reduce.12.cloned.1.call-done = f32[8,6144]{1,0:T(8,128)} async-done(((f32[8,6144]{1,0:T(8,128)}), f32[8,6144]{1,0:T(8,128)}) %all-reduce.12.cloned.1.call-update) | async-done | bytes 196624 | tf_op jit(solution)/shard_map/psum | solution.py:66
  212.2 22.2 %all-reduce = (f32[8]{0:T(128)S(1)}, f32[8]{0:T(128)S(1)}) all-reduce(f32[8]{0:T(128)S(1)} %get-tuple-element.11, f32[8]{0:T(128)S(1)} %get-tuple-element.10), channel_id=1, replica_groups=mesh['sub'=8,'coarse'=4] {'sub'}, use_global_device_ids=true, to_apply=%region_3.4 | all-reduce | flops 16 | bytes 128 | tf_op jit(solution)/shard_map/psum | solution.py:71
  245.1 22.9 %gather_fusion.3 = f32[6144,8]{1,0:T(8,128)} fusion(f32[8,6144]{0,1:T(8,128)S(1)} %copy.209, s32[6144]{0:T(1024)} %copy-done.3), kind=kCustom, calls=%fused_computation.3 | custom fusion | bytes 417792 | tf_op jit(solution)/shard_map/gather | solution.py:50
  275.1 9.9 scatter_custom_fusion.2
  286.8 28.2 %all-reduce.14.cloned.1.call-done = f32[8,6144]{1,0:T(8,128)} async-done(((f32[8,6144]{1,0:T(8,128)}), f32[8,6144]{1,0:T(8,128)}) %all-reduce.14.cloned.1.call-update) | async-done | bytes 196624 | tf_op jit(solution)/shard_map/psum | solution.py:66
  323.4 22.3 %psum.146 = f32[8]{0:T(128)S(1)} all-reduce(f32[8]{0:T(128)S(1)} %multiply_reduce_fusion.5), channel_id=1, replica_groups=mesh['sub'=8,'coarse'=4] {'sub'}, use_global_device_ids=true, to_apply=%region_12.13 | all-reduce | flops 8 | bytes 64 | tf_op jit(solution)/shard_map/psum | solution.py:71
  356.8 22.9 %gather_fusion.4 = f32[6144,8]{1,0:T(8,128)} fusion(f32[8,6144]{0,1:T(8,128)S(1)} %copy.213, s32[6144]{0:T(1024)} %copy-done.3), kind=kCustom, calls=%fused_computation.4 | custom fusion | bytes 417792 | tf_op jit(solution)/shard_map/gather | solution.py:50
  386.2 17.1 %psum.147 = f32[8,64]{1,0:T(8,128)S(1)} all-reduce(f32[8,64]{1,0:T(8,128)S(1)} %fusion.42), channel_id=1, replica_groups=mesh['sub'=8,'coarse'=4] {'sub'}, use_global_device_ids=true, to_apply=%region_13.14 | all-reduce | flops 512 | bytes 4096 | tf_op jit(solution)/shard_map/psum | solution.py:42
  422.5 29.6 %all-reduce.16.cloned.1.call-done = f32[8,6144]{1,0:T(8,128)} async-done(((f32[8,6144]{1,0:T(8,128)}), f32[8,6144]{1,0:T(8,128)}) %all-reduce.16.cloned.1.call-update) | async-done | bytes 196624 | tf_op jit(solution)/shard_map/psum | solution.py:66
  460.5 22.2 %psum.149 = f32[8]{0:T(128)S(1)} all-reduce(f32[8]{0:T(128)S(1)} %multiply_reduce_fusion.4), channel_id=1, replica_groups=mesh['sub'=8,'coarse'=4] {'sub'}, use_global_device_ids=true, to_apply=%region_17.18 | all-reduce | flops 8 | bytes 64 | tf_op jit(solution)/shard_map/psum | solution.py:80
  494.0 22.9 %gather_fusion.6 = f32[6144,8]{1,0:T(8,128)} fusion(f32[8,6144]{0,1:T(8,128)S(1)} %copy.220, s32[6144]{0:T(1024)} %copy-done.3), kind=kCustom, calls=%fused_computation.6 | custom fusion | bytes 417792 | tf_op jit(solution)/shard_map/gather | solution.py:50
  535.7 28.0 %all-reduce.18.cloned.1.call-done = f32[8,6144]{1,0:T(8,128)} async-done(((f32[8,6144]{1,0:T(8,128)}), f32[8,6144]{1,0:T(8,128)}) %all-reduce.18.cloned.1.call-update) | async-done | bytes 196624 | tf_op jit(solution)/shard_map/psum | solution.py:66
  572.2 22.3 %psum.151 = f32[8]{0:T(128)S(1)} all-reduce(f32[8]{0:T(128)S(1)} %multiply_reduce_fusion.3), channel_id=1, replica_groups=mesh['sub'=8,'coarse'=4] {'sub'}, use_global_device_ids=true, to_apply=%region_21.22 | all-reduce | flops 8 | bytes 64 | tf_op jit(solution)/shard_map/psum | solution.py:71
  605.6 22.9 %gather_fusion.7 = f32[6144,8]{1,0:T(8,128)} fusion(f32[8,6144]{0,1:T(8,128)S(1)} %copy.224, s32[6144]{0:T(1024)} %copy-done.3), kind=kCustom, calls=%fused_computation.7 | custom fusion | bytes 417792 | tf_op jit(solution)/shard_map/gather | solution.py:50
  634.9 17.1 %psum.152 = f32[8,64]{1,0:T(8,128)S(1)} all-reduce(f32[8,64]{1,0:T(8,128)S(1)} %fusion.41), channel_id=1, replica_groups=mesh['sub'=8,'coarse'=4] {'sub'}, use_global_device_ids=true, to_apply=%region_22.23 | all-reduce | flops 512 | bytes 4096 | tf_op jit(solution)/shard_map/psum | solution.py:42
  659.5 9.9 scatter_custom_fusion.5
  671.3 29.6 %all-reduce.20.cloned.1.call-done = f32[8,6144]{1,0:T(8,128)} async-done(((f32[8,6144]{1,0:T(8,128)}), f32[8,6144]{1,0:T(8,128)}) %all-reduce.20.cloned.1.call-update) | async-done | bytes 196624 | tf_op jit(solution)/shard_map/psum | solution.py:66
  709.2 22.2 %psum.154 = f32[8]{0:T(128)S(1)} all-reduce(f32[8]{0:T(128)S(1)} %multiply_reduce_fusion.2), channel_id=1, replica_groups=mesh['sub'=8,'coarse'=4] {'sub'}, use_global_device_ids=true, to_apply=%region_26.27 | all-reduce | flops 8 | bytes 64 | tf_op jit(solution)/shard_map/psum | solution.py:80
  742.9 22.9 %gather_fusion.9 = f32[6144,8]{1,0:T(8,128)} fusion(f32[8,6144]{0,1:T(8,128)S(1)} %copy.231, s32[6144]{0:T(1024)} %copy-done.3), kind=kCustom, calls=%fused_computation.9 | custom fusion | bytes 417792 | tf_op jit(solution)/shard_map/gather | solution.py:50
  784.6 28.0 %all-reduce.22.cloned.1.call-done = f32[8,6144]{1,0:T(8,128)} async-done(((f32[8,6144]{1,0:T(8,128)}), f32[8,6144]{1,0:T(8,128)}) %all-reduce.22.cloned.1.call-update) | async-done | bytes 196624 | tf_op jit(solution)/shard_map/psum | solution.py:66
  821.1 22.3 %psum.156 = f32[8]{0:T(128)S(1)} all-reduce(f32[8]{0:T(128)S(1)} %multiply_reduce_fusion.1), channel_id=1, replica_groups=mesh['sub'=8,'coarse'=4] {'sub'}, use_global_device_ids=true, to_apply=%region_30.31 | all-reduce | flops 8 | bytes 64 | tf_op jit(solution)/shard_map/psum | solution.py:71
  854.5 22.9 %gather_fusion.10 = f32[6144,8]{1,0:T(8,128)} fusion(f32[8,6144]{0,1:T(8,128)S(1)} %copy.235, s32[6144]{0:T(1024)} %copy-done.3), kind=kCustom, calls=%fused_computation.10 | custom fusion | bytes 417792 | tf_op jit(solution)/shard_map/gather | solution.py:50
  883.9 17.1 %psum.157 = f32[8,64]{1,0:T(8,128)S(1)} all-reduce(f32[8,64]{1,0:T(8,128)S(1)} %fusion.40), channel_id=1, replica_groups=mesh['sub'=8,'coarse'=4] {'sub'}, use_global_device_ids=true, to_apply=%region_31.32 | all-reduce | flops 512 | bytes 4096 | tf_op jit(solution)/shard_map/psum | solution.py:42
  908.5 9.9 scatter_custom_fusion.7
  920.2 29.6 %all-reduce.24.cloned.1.call-done = f32[8,6144]{1,0:T(8,128)} async-done(((f32[8,6144]{1,0:T(8,128)}), f32[8,6144]{1,0:T(8,128)}) %all-reduce.24.cloned.1.call-update) | async-done | bytes 196624 | tf_op jit(solution)/shard_map/psum | solution.py:66
  958.2 22.2 %psum.159 = f32[8]{0:T(128)S(1)} all-reduce(f32[8]{0:T(128)S(1)} %multiply_reduce_fusion), channel_id=1, replica_groups=mesh['sub'=8,'coarse'=4] {'sub'}, use_global_device_ids=true, to_apply=%region_35.36 | all-reduce | flops 8 | bytes 64 | tf_op jit(solution)/shard_map/psum | solution.py:80
  (248 shorter events, 285.9 us)
Async XLA Ops:
  7.2 126.0 %copy-start = (bf16[4,24,1536]{2,1,0:T(8,128)(2,1)S(1)}, bf16[4,24,1536]{2,1,0:T(8,128)(2,1)}, u32[]{:S(2)}) copy-start(bf16[4,24,1536]{2,1,0:T(8,128)(2,1)} %param.10) | copy-start | bytes 884740
  7.2 82.8 %all-reduce.10.cloned.1.call-start = ((), (), s32[]{:S(2)}) async-start(), calls=%async_computation | async-start | bytes 393216 | tf_op jit(solution)/shard_map/psum | solution.py:66
  8.2 8.1 collective-permute-start
  11.9 30.9 %copy-start.3 = (s32[6144]{0:T(1024)}, s32[6144]{0:T(1024)S(1)}, u32[]{:S(2)}) copy-start(s32[6144]{0:T(1024)S(1)} %broadcast_clamp_fusion) | copy-start | bytes 73732
  12.0 35.7 %copy-start.12 = (s32[1536]{0:T(1024)}, s32[1536]{0:T(1024)S(1)}, u32[]{:S(2)}) copy-start(s32[1536]{0:T(1024)S(1)} %fusion.69) | copy-start | bytes 18436
  47.7 47.4 %copy-start.13 = (s32[4,24]{1,0:T(4,128)S(1)}, s32[4,24]{1,0:T(4,128)}, u32[]{:S(2)}) copy-start(s32[4,24]{1,0:T(4,128)} %param.13) | copy-start | bytes 1156
  59.4 144.4 %all-reduce.12.cloned.1.call-start = ((), (), s32[]{:S(2)}) async-start(), calls=%async_computation.1 | async-start | bytes 393216 | tf_op jit(solution)/shard_map/psum | solution.py:66
  90.8 6.5 collective-permute-start.1
  98.2 7.2 collective-permute-start.2
  175.6 139.4 %all-reduce.14.cloned.1.call-start = ((), (), s32[]{:S(2)}) async-start(), calls=%async_computation.2 | async-start | bytes 393216 | tf_op jit(solution)/shard_map/psum | solution.py:66
  204.6 6.5 collective-permute-start.3
  235.5 7.0 collective-permute-start.4
  286.8 165.3 %all-reduce.16.cloned.1.call-start = ((), (), s32[]{:S(2)}) async-start(), calls=%async_computation.3 | async-start | bytes 393216 | tf_op jit(solution)/shard_map/psum | solution.py:66
  315.9 6.5 collective-permute-start.5
  347.4 6.8 collective-permute-start.6
  422.4 141.3 %all-reduce.18.cloned.1.call-start = ((), (), s32[]{:S(2)}) async-start(), calls=%async_computation.4 | async-start | bytes 393216 | tf_op jit(solution)/shard_map/psum | solution.py:66
  452.9 6.5 collective-permute-start.7
  484.3 7.1 collective-permute-start.8
  535.7 165.1 %all-reduce.20.cloned.1.call-start = ((), (), s32[]{:S(2)}) async-start(), calls=%async_computation.5 | async-start | bytes 393216 | tf_op jit(solution)/shard_map/psum | solution.py:66
  564.7 6.5 collective-permute-start.9
  596.2 6.8 collective-permute-start.10
  671.2 141.4 %all-reduce.22.cloned.1.call-start = ((), (), s32[]{:S(2)}) async-start(), calls=%async_computation.6 | async-start | bytes 393216 | tf_op jit(solution)/shard_map/psum | solution.py:66
  701.7 6.5 collective-permute-start.11
  733.2 7.1 collective-permute-start.12
  784.6 165.2 %all-reduce.24.cloned.1.call-start = ((), (), s32[]{:S(2)}) async-start(), calls=%async_computation.7 | async-start | bytes 393216 | tf_op jit(solution)/shard_map/psum | solution.py:66
  813.5 6.5 collective-permute-start.13
  845.1 6.8 collective-permute-start.14
  908.5 72.0 %copy-start.27 = (f32[8]{0:T(128)S(1)}, f32[8]{0:T(128)}, u32[]{:S(2)}) copy-start(f32[8]{0:T(128)} %copy-done.26) | copy-start | bytes 100
  908.5 72.0 %copy-start.15 = (f32[8]{0:T(128)S(1)}, f32[8]{0:T(128)}, u32[]{:S(2)}) copy-start(f32[8]{0:T(128)} %copy-done.14) | copy-start | bytes 100
  908.5 72.0 %copy-start.17 = (f32[8]{0:T(128)S(1)}, f32[8]{0:T(128)}, u32[]{:S(2)}) copy-start(f32[8]{0:T(128)} %copy-done.16) | copy-start | bytes 100
  908.5 72.0 %copy-start.19 = (f32[8]{0:T(128)S(1)}, f32[8]{0:T(128)}, u32[]{:S(2)}) copy-start(f32[8]{0:T(128)} %copy-done.18) | copy-start | bytes 100
  950.7 6.5 collective-permute-start.15
  (21 other events, 202.9 us)
Sparse Core Ops, SparseCore 0:
  59.5 30.3 all-reduce.9
  175.7 27.9 all-reduce.11
  286.9 28.0 all-reduce.13
  422.6 29.4 all-reduce.15
  535.8 27.9 all-reduce.17
  671.3 29.4 all-reduce.19
  784.7 27.9 all-reduce.21
  920.3 29.4 all-reduce.23
where the time goes:
time: 1000 us; the launch traced here: 990 us
  waiting for transfers between devices  299 us (30%)
  local copies, waits for them, and re-layouts  250 us (25%)
  blocking collectives  247 us (25%)
  other arithmetic  107 us (11%)
  starting transfers between devices  38.8 us (4%)
  matrix products  31.8 us (3%)
  between operations  15.2 us (2%)
    psum x8, waiting for transfers between devices, apply_operator(): sums = lax.psum(sums, 'coarse')  232 us
    gather x16, local copies, waits for them, and re-layouts, apply_operator(): gathered = (window[:, local_pos] * signs).astype(jnp.bfloat16)  200 us
    psum x4, blocking collectives, fit_of(): return lax.psum(jnp.sum(residual * pre, axis=1), 'sub')  89.2 us
    scatter-add x8, other arithmetic, apply_operator(): sums = jnp.zeros((cases, lam_rows + lam_rows), jnp.float32).at[:, block_p...  79 us
    psum x4, blocking collectives, coarse_answer(): load = lax.psum(partial_load, 'sub')  70.6 us
    ppermute x16, waiting for transfers between devices, passed_along(): return lax.ppermute(value, axis, pairs)  67.7 us
    psum x3, blocking collectives, per_device(): alpha = fit / lax.psum(jnp.sum(direction * image, axis=1), 'sub')  66.6 us
    ppermute x16, starting transfers between devices, passed_along(): return lax.ppermute(value, axis, pairs)  38.5 us
  transfers between devices with their start and end apart: 24, of which 24 were waited for; matrix products, arithmetic and copies ran while one was open for 0% of the time, Pallas kernels for 0%

commit v1 on v0

v1 whole, which is shorter than its diff:
```python
import functools

import jax
import jax.numpy as jnp
from jax import lax
from jax.experimental import pallas as pl
from jax.experimental.pallas import tpu as pltpu
from jax.sharding import PartitionSpec as P

ITERS = 4
LANES = 128
HIGH = lax.Precision.HIGHEST
MESH = pl.DeviceIdType.MESH
NT = (((1,), (1,)), ((), ()))


def passed_along(value, axis, steps):
    count = lax.axis_size(axis)
    pairs = [(source, (source + steps) % count) for source in range(count)]
    return lax.ppermute(value, axis, pairs)


def search(want_ref, col_ref, out_ref, width):
    group = 4 if (width // LANES) % 4 == 0 else 1
    span = group * LANES
    rows = col_ref.shape[0] // 8

    def outer(g, carry):
        want = [
            jnp.broadcast_to(
                want_ref[:, pl.ds(pl.multiple_of(g * span + i * LANES, LANES), LANES)], (8, LANES)
            )
            for i in range(group)
        ]

        def inner(k, accs):
            for u in range(8):
                row = k * 8 + u
                col = col_ref[pl.ds(pl.multiple_of(row * 8, 8), 8), :]
                accs = tuple(jnp.where(col == w, row, a) for w, a in zip(want, accs))
            return accs

        start = tuple(jnp.full((8, LANES), -1, jnp.int32) for _ in range(group))
        accs = lax.fori_loop(0, rows // 8, inner, start)
        sub = lax.broadcasted_iota(jnp.int32, (8, LANES), 0)
        for i in range(group):
            pos = jnp.max(accs[i] * 8 + sub, axis=0, keepdims=True)
            out_ref[:, pl.ds(pl.multiple_of(g * span + i * LANES, LANES), LANES)] = (
                jnp.broadcast_to(pos, (8, LANES))
            )
        return carry

    lax.fori_loop(0, width // span, outer, 0)


def search_kernel(first_ref, second_ref, own_ref, col_s_ref, col_f_ref, q1_ref, q2_ref, qo_ref):
    lam = own_ref.shape[1]
    search(first_ref, col_s_ref, q1_ref, lam)
    search(second_ref, col_f_ref, q2_ref, lam)
    search(own_ref, col_f_ref.at[pl.ds(0, lam)], qo_ref, lam)


def iterate_kernel(
    n_sub, rhs_ref, prev_ref, dual_ref, precond_ref, corner_ref, block_corner_ref, table_ref,
    kinv_ref, q1_ref, q2_ref, w1_ref, w2_ref, qo_ref,
    lam_out, res_out,
    D, R, L, V, S, rx, dtx, drx, ltx, lrx, ssem, rsem, dssem, drsem, lssem, lrsem,
):
    j = lax.axis_index("sub")
    c = lax.axis_index("coarse")
    subs, br, order = dual_ref.shape
    bw = subs * br
    half = 2 * bw
    hw = bw // 2
    right = lax.rem(j + 1, n_sub)
    left = lax.rem(j + n_sub - 1, n_sub)
    high = c // 2
    halo = lax.rem(j + 1 - 2 * high + n_sub, n_sub)
    halo_slot = 6 + c - 4 * high
    peers = [(j, lax.rem(c + o, 4)) for o in range(1, 4)]

    barrier = pltpu.get_barrier_semaphore()
    friends = list(peers)
    for o in range(4):
        friends += [(left, o), (right, o)]
    for o in range(2, n_sub - 1):
        friends.append((lax.rem(j + o, n_sub), c))
    for f in friends:
        pl.semaphore_signal(barrier, inc=1, device_id=f, device_id_type=MESH)
    pl.semaphore_wait(barrier, len(friends))

    def gather(idx_ref, src_ref, count, finish):
        def body(o, carry):
            at = pl.ds(pl.multiple_of(o * LANES, LANES), LANES)
            idx = idx_ref[:, at]
            lo = jnp.bitwise_and(idx, LANES - 1)
            hi = jnp.right_shift(idx, 7)
            acc = jnp.zeros((8, LANES), jnp.float32)
            for k in range(count):
                got = jnp.take_along_axis(
                    src_ref[:, k * LANES : (k + 1) * LANES], lo, axis=1,
                    mode="promise_in_bounds",
                )
                acc = jnp.where(hi == k, got, acc)
            finish(o, acc)
            return carry

        lax.fori_loop(0, half // LANES, body, 0)

    def put(ref, base, scale=None):
        def finish(o, acc):
            at = pl.ds(pl.multiple_of(base + o * LANES, LANES), LANES)
            ref[:, at] = acc

        return finish

    S[:, :half] = rhs_ref[...]
    S[:, half : 2 * half] = prev_ref[...]
    steps = half // LANES
    gather(w1_ref, S, 2 * steps, put(R, 0))
    gather(w2_ref, S, 2 * steps, put(R, half))
    D[...] = jnp.zeros_like(D)
    L[...] = jnp.zeros_like(L)

    def gathered(ref, s):
        parts = []
        for b in range(4):
            part = ref[:, b * bw + s * br : b * bw + (s + 1) * br]
            parts.append(part if b < 2 else -part)
        return jnp.concatenate(parts, axis=1).astype(jnp.bfloat16)

    def unpack(block):
        wide = block.astype(jnp.float32)
        return jnp.concatenate([wide[:8], wide[8:]], axis=1)

    def exchange(app, terms, vec_ref):
        rx[app, 0] = jnp.concatenate([terms[:, :hw], terms[:, hw:]], axis=0).astype(jnp.bfloat16)
        copies = []
        for i in range(7):
            if i < 3:
                slot, device = i + 1, peers[i]
            else:
                slot, device = halo_slot, (halo, i - 3)
            copy = pltpu.make_async_remote_copy(
                src_ref=rx.at[app, 0], dst_ref=rx.at[app, slot],
                send_sem=ssem.at[i], recv_sem=rsem.at[app, slot - 1],
                device_id=device, device_id_type=MESH,
            )
            copy.start()
            copies.append(copy)
        for slot in range(1, 8):
            pltpu.make_async_copy(
                rx.at[app, slot], rx.at[app, slot], rsem.at[app, slot - 1]
            ).wait()
        blocks = [unpack(rx[app, lax.rem(c + 4 - b, 4)]) for b in range(4)]
        part = jnp.zeros((8, LANES), jnp.float32)
        for b in range(4):
            prod = vec_ref[:, b * bw : (b + 1) * bw] * blocks[b]
            for k in range(bw // LANES):
                piece = prod[:, k * LANES : (k + 1) * LANES]
                part = part + piece if b < 2 else part - piece
        dtx[app] = part
        dots = []
        for o in range(1, n_sub):
            copy = pltpu.make_async_remote_copy(
                src_ref=dtx.at[app], dst_ref=drx.at[app, o - 1],
                send_sem=dssem.at[o - 1], recv_sem=drsem.at[app],
                device_id=(lax.rem(j + o, n_sub), c), device_id_type=MESH,
            )
            copy.start()
            dots.append(copy)
        V[:, :bw] = blocks[0]
        V[:, bw:half] = blocks[1]
        V[:, half : half + bw] = blocks[2]
        V[:, half + bw :] = blocks[3]
        S[:, :bw] = blocks[2]
        S[:, bw:half] = blocks[3]
        S[:, half : half + bw] = unpack(rx[app, 4])
        S[:, half + bw : 2 * half] = unpack(rx[app, 5])

        def less(o, acc):
            at = pl.ds(pl.multiple_of(o * LANES, LANES), LANES)
            S_first[:, at] = V[:, at]
            V[:, at] = V[:, at] - acc

        def more(o, acc):
            at = pl.ds(pl.multiple_of(half + o * LANES, LANES), LANES)
            V[:, at] = acc - V[:, at]

        S_first = S.at[:, pl.ds(2 * half, half)]
        gather(q1_ref, S, 2 * steps, less)
        S[:, :half] = S[:, 2 * half :]
        S[:, half : half + bw] = unpack(rx[app, 6])
        S[:, half + bw : 2 * half] = unpack(rx[app, 7])
        gather(q2_ref, S, 2 * steps, more)
        pltpu.make_async_copy(drx.at[app], drx.at[app], drsem.at[app]).wait()
        total = part
        for o in range(n_sub - 1):
            total = total + drx[app, o]
        for copy in copies + dots:
            copy.wait_send()
        return jnp.sum(total, axis=1, keepdims=True)

    def product(ops_ref, vecs):
        return [
            lax.dot_general(vecs[s], ops_ref[s], NT, preferred_element_type=jnp.float32)
            for s in range(subs)
        ]

    def body(step, fit):
        vecs = [gathered(R, s) for s in range(subs)]
        terms = jnp.concatenate(product(precond_ref, vecs), axis=1)
        fit_next = exchange(2 * step, terms, R)
        D[...] = V[...] + (fit_next / fit) * D[...]

        vecs = [gathered(D, s) for s in range(subs)]
        load = jnp.zeros((8, kinv_ref.shape[0]), jnp.float32)
        for s in range(subs):
            lifted = lax.dot_general(
                vecs[s], corner_ref[s], NT, preferred_element_type=jnp.float32
            )
            load = load + jnp.dot(
                lifted, table_ref[s], precision=HIGH, preferred_element_type=jnp.float32
            )
        ltx[step] = load
        loads = []
        for o in range(1, n_sub):
            copy = pltpu.make_async_remote_copy(
                src_ref=ltx.at[step], dst_ref=lrx.at[step, o - 1],
                send_sem=lssem.at[o - 1], recv_sem=lrsem.at[step],
                device_id=(lax.rem(j + o, n_sub), c), device_id_type=MESH,
            )
            copy.start()
            loads.append(copy)
        outs = product(dual_ref, vecs)
        pltpu.make_async_copy(lrx.at[step], lrx.at[step], lrsem.at[step]).wait()
        for o in range(n_sub - 1):
            load = load + lrx[step, o]
        answer = lax.dot_general(
            load, kinv_ref[...], NT, precision=HIGH, preferred_element_type=jnp.float32
        ).astype(jnp.bfloat16)
        wide = answer.astype(jnp.float32)
        for s in range(subs):
            spread = lax.dot_general(
                wide, table_ref[s], NT, preferred_element_type=jnp.float32
            ).astype(jnp.bfloat16)
            outs[s] = outs[s] + jnp.dot(
                spread, block_corner_ref[s], preferred_element_type=jnp.float32
            )
        energy = exchange(2 * step + 1, jnp.concatenate(outs, axis=1), D)
        for copy in loads:
            copy.wait_send()
        alpha = fit_next / energy
        L[...] = L[...] + alpha * D[:, :half]
        R[...] = R[...] - alpha * V[...]
        return fit_next

    lax.fori_loop(0, ITERS, body, jnp.ones((8, 1), jnp.float32))
    gather(qo_ref, L, steps, put(lam_out, 0))
    gather(qo_ref, R, steps, put(res_out, 0))


def per_device(
    right_side, dual_ops, precond_ops, corner_ops, coarse_inverse, sub_index, corner_map
):
    cases, lam = right_side.shape
    subs, br, order = dual_ops.shape
    ncg = coarse_inverse.shape[1]
    n_sub = lax.axis_size("sub")
    here = lax.axis_index("sub")
    mine = lax.axis_index("coarse")
    total = lam * n_sub
    slots = sub_index.reshape(subs, 4, br).transpose(1, 0, 2).reshape(-1)
    first, second = slots[:lam], slots[lam:]
    first_prev = passed_along(first, "sub", 1)
    second_next = passed_along(second, "sub", -1)
    prev = passed_along(right_side, "sub", 1)
    kinv = lax.all_gather(coarse_inverse, "coarse", axis=0, tiled=True)
    pad = -ncg % LANES
    kinv = jnp.pad(kinv, ((0, pad), (0, pad)))
    own = jnp.arange(lam, dtype=jnp.int32) + here * lam
    wide = lambda x: jnp.broadcast_to(x[:, None], (x.shape[0], LANES))
    col_s = wide(jnp.concatenate([second, second_next]))
    col_f = wide(jnp.concatenate([first, first_prev]))
    index = jax.ShapeDtypeStruct((8, lam), jnp.int32)
    vmem = pl.BlockSpec(memory_space=pltpu.VMEM)
    q1, q2, qo = pl.pallas_call(
        search_kernel,
        out_shape=[index] * 3,
        in_specs=[vmem] * 5,
        out_specs=[vmem] * 3,
        compiler_params=pltpu.CompilerParams(vmem_limit_bytes=32 * 2**20),
        name="search",
    )(first[None], second[None], own[None], col_s, col_f)
    spot = lambda x: jnp.broadcast_to(
        jnp.mod(x - here * lam + total, total)[None], (8, lam)
    )
    w1 = spot(first)
    w2 = spot(second)
    w2 = jnp.where(w2 < lam, w2, w2 - (total - lam) + lam)
    table = (corner_map[:, :, None] == jnp.arange(ncg + pad)[None, None, :]).astype(jnp.float32)
    block_corner = lax.dynamic_slice_in_dim(corner_ops, mine * br, br, 2)
    bw = subs * br
    f32 = lambda *dims: pltpu.VMEM(dims, jnp.float32)
    dma = pltpu.SemaphoreType.DMA
    out = jax.ShapeDtypeStruct((cases, lam), jnp.float32)
    return pl.pallas_call(
        functools.partial(iterate_kernel, n_sub),
        out_shape=[out, out],
        in_specs=[vmem] * 13,
        out_specs=[vmem] * 2,
        scratch_shapes=[
            f32(8, 2 * lam), f32(8, 2 * lam), f32(8, lam), f32(8, 2 * lam), f32(8, 3 * lam),
            pltpu.VMEM((2 * ITERS, 8, 16, bw // 2), jnp.bfloat16),
            f32(2 * ITERS, 8, LANES), f32(2 * ITERS, n_sub - 1, 8, LANES),
            f32(ITERS, 8, ncg + pad), f32(ITERS, n_sub - 1, 8, ncg + pad),
            dma((7,)), dma((2 * ITERS, 7)),
            dma((n_sub - 1,)), dma((2 * ITERS,)),
            dma((n_sub - 1,)), dma((ITERS,)),
        ],
        compiler_params=pltpu.CompilerParams(
            collective_id=0, has_side_effects=True, vmem_limit_bytes=40 * 2**20
        ),
        name="iterate",
    )(
        right_side, prev, dual_ops, precond_ops, corner_ops, block_corner, table,
        kinv, q1, q2, w1, w2, qo,
    )


def solution(mesh):
    placed = (
        P(None, "sub"),
        P("sub", "coarse", None),
        P("sub", "coarse", None),
        P("sub", None, None),
        P("coarse", None),
        P("sub", None),
        P("sub", None),
    )
    return jax.shard_map(
        per_device,
        mesh=mesh,
        in_specs=placed,
        out_specs=(P(None, "sub"), P(None, "sub")),
        check_vma=False,
    )
```

time: 1000 us -> 174 us (0.17); the launches traced: 990 us -> 174 us
  waiting for transfers between devices: 299 us -> 0.01 us
  local copies, waits for them, and re-layouts: 250 us -> 4.81 us
  blocking collectives: 247 us -> 5.41 us
  Pallas kernels: 0 us -> 156 us
  other arithmetic: 107 us -> 0.84 us
  starting transfers between devices: 38.8 us -> 6.12 us
  matrix products: 31.8 us -> 0 us
  between operations: 15.2 us -> 0.89 us
    psum x8 -> x0, waiting for transfers between devices: 232 us -> none  [apply_operator(): sums = lax.psum(sums, 'coarse')]
    psum x11 -> x0, blocking collectives: 226 us -> none  [the longest x4 89.2 us: fit_of(): return lax.psum(jnp.sum(residual * pre, axis=1), 'sub')]
    gather x24 -> x0, local copies, waits for them, and re-layouts: 203 us -> none  [the longest x16 200 us: apply_operator(): gathered = (window[:, local_pos] * signs).astype(jnp.bfloat16)]
    pallas_call x0 -> x2, Pallas kernels: none -> 156 us  [the longest x1 138 us: per_device(): pl.pallas_call(functools.partial(iterate_kernel, n_sub), out_shape=[out,...]
    scatter-add x8 -> x0, other arithmetic: 79 us -> none  [apply_operator(): sums = jnp.zeros((cases, lam_rows + lam_rows), jnp.float32).at[:, block_p...]
    ppermute x16 -> x3, waiting for transfers between devices: 67.7 us -> 0.01 us  [passed_along(): return lax.ppermute(value, axis, pairs)]
    ppermute x16 -> x3, starting transfers between devices: 38.5 us -> 6.12 us  [passed_along(): return lax.ppermute(value, axis, pairs)]
    dot_general x24 -> x0, matrix products: 31.8 us -> none  [the longest x8 29.2 us: apply_operator(): jnp.einsum('smn,ksn->ksm', matrices, gathered, preferred_element_type=jnp...]
  transfers between devices with their start and end apart: 24 -> 3, of which waited for: 24 -> 0; matrix products, arithmetic and copies ran while one was open for 0% -> 2% of each run, Pallas kernels for 0% -> 10%
where the time goes in v1:
time: 174 us
  Pallas kernels  156 us (90%)
  starting transfers between devices  6.12 us (4%)
  blocking collectives  5.41 us (3%)
  local copies, waits for them, and re-layouts  4.81 us (3%)
    pallas_call x1, Pallas kernels, per_device(): pl.pallas_call(functools.partial(iterate_kernel, n_sub), out_shape=[out,...  138 us
    pallas_call x1, Pallas kernels, per_device(): pl.pallas_call(search_kernel, out_shape=[index] * 3, in_specs=[vmem] * 5,...  17.7 us
    ppermute x3, starting transfers between devices, passed_along(): return lax.ppermute(value, axis, pairs)  6.12 us
    all_gather x1, blocking collectives, per_device(): kinv = lax.all_gather(coarse_inverse, 'coarse', axis=0, tiled=True)  5.41 us
  transfers between devices with their start and end apart: 3, of which 0 were waited for; matrix products, arithmetic and copies ran while one was open for 2% of the time, Pallas kernels for 10%

profile of v1, /device:TPU:0, one launch (start us, length us, event | category | flops | bytes accessed | tf_op | source)
XLA Modules:
  0.0 174.0 jit_solution(378017809156572192)
XLA Ops:
  0.6 0.7 fusion.1
  1.4 6.1 %collective-permute-start.1 = (s32[3072]{0:T(1024)S(1)}, s32[3072]{0:T(1024)S(1)}, u32[]{:S(2)}, u32[]{:S(2)}) collective-permute-start(s32[3072]{0:T(1024)S(1)} %slice.14), channel_id=1, source_target_pairs={{0,28},{4,0},{8,4},{12,8},{16,12},{20,16},{24,20},{28,24},{1,29},{... | collective-permute-start | bytes 36872 | tf_op jit(solution)/shard_map/ppermute | solution.py:20
  7.4 0.0 collective-permute-start.2
  7.4 0.1 collective-permute-start
  7.6 0.8 fusion.table_ref
  8.4 0.0 slice-start.2
  8.4 1.0 constant_dynamic-slice_fusion.block_corner_ref
  9.4 5.4 %all_gather.3 = f32[64,64]{1,0:T(8,128)S(1)} all-gather(f32[16,64]{1,0:T(8,128)} %param.11), channel_id=1, replica_groups=mesh['sub'=8,'coarse'=4] {'coarse'}, dimensions={0}, use_global_device_ids=true | all-gather | bytes 20480 | tf_op jit(solution)/shard_map/all_gather | solution.py:278
  14.8 0.0 slice-start
  14.8 0.0 collective-permute-done.1
  14.9 0.0 collective-permute-done.2
  14.9 0.9 broadcast_in_dim.18.col_s_ref
  15.7 0.0 slice-start.1
  15.8 0.0 slice-start.3
  15.8 0.0 copy-start
  15.8 0.0 copy-start.1
  15.8 0.9 broadcast_in_dim.19.col_f_ref
  16.7 17.7 %search.1 = (s32[8,3072]{1,0:T(8,128)S(1)}, s32[8,3072]{1,0:T(8,128)S(1)}, s32[8,3072]{1,0:T(8,128)S(1)}) custom-call(s32[1,3072]{1,0:T(1,128)S(1)} %broadcast_in_dim.16.first_ref, s32[1,3072]{1,0:T(1,128)S(1)} %broadcast_in_dim.17.second_ref, s32[1,3072]{1,0:T(1,128)S(1)} %iota_add_fusion.own_ref, s32[6144,128]{1,0:T(8,128)S(1)} %broadcast_in_dim.18.col_s_ref, ...), custom_call_target="tpu_custom_call" | custom-call | tf_op jit(solution)/shard_map/search/pallas_call | solution.py:287
  34.4 0.0 collective-permute-done.prev_ref
  34.4 0.0 slice-done.2
  34.4 0.0 slice-done
  34.4 0.0 slice-done.1
  34.4 0.0 slice-done.3
  34.4 0.0 copy-done
  34.4 0.0 copy-done.1
  34.5 138.3 %iterate.1 = (f32[8,3072]{1,0:T(8,128)S(1)}, f32[8,3072]{1,0:T(8,128)S(1)}) custom-call(f32[8,3072]{1,0:T(8,128)S(1)} %copy-done.1, f32[8,3072]{1,0:T(8,128)S(1)} %collective-permute-done.prev_ref, bf16[4,384,1536]{2,1,0:T(8,128)(2,1)S(1)} %bitcast.4, bf16[4,384,1536]{2,1,0:T(8,128)(2,1)S(1)} %bitcast.6, bf16[4,24,1536]{2,1,0:T(8,128)(2,1)S(1)} %copy-done, ...), custom_call_target="tpu_custom_call" | custom-call | tf_op jit(solution)/shard_map/iterate/pallas_call | solution.py:307
  172.7 0.6 copy.12
  173.4 0.6 copy.13
  (15 shorter events, 0.2 us)
Async XLA Ops:
  1.4 13.5 %collective-permute-start.1 = (s32[3072]{0:T(1024)S(1)}, s32[3072]{0:T(1024)S(1)}, u32[]{:S(2)}, u32[]{:S(2)}) collective-permute-start(s32[3072]{0:T(1024)S(1)} %slice.14), channel_id=1, source_target_pairs={{0,28},{4,0},{8,4},{12,8},{16,12},{20,16},{24,20},{28,24},{1,29},{... | collective-permute-start | bytes 36872 | tf_op jit(solution)/shard_map/ppermute | solution.py:20
  7.4 7.4 %collective-permute-start.2 = (s32[3072]{0:T(1024)S(1)}, s32[3072]{0:T(1024)S(1)}, u32[]{:S(2)}, u32[]{:S(2)}) collective-permute-start(s32[3072]{0:T(1024)S(1)} %slice.15), channel_id=1, source_target_pairs={{0,4},{4,8},{8,12},{12,16},{16,20},{20,24},{24,28},{28,0},{1,5},{5... | collective-permute-start | bytes 36872 | tf_op jit(solution)/shard_map/ppermute | solution.py:20
  7.4 26.9 %collective-permute-start = (f32[8,3072]{1,0:T(8,128)}, f32[8,3072]{1,0:T(8,128)S(1)}, u32[]{:S(2)}, u32[]{:S(2)}) collective-permute-start(f32[8,3072]{1,0:T(8,128)} %rhs_ref.1), channel_id=1, source_target_pairs={{0,4},{4,8},{8,12},{12,16},{16,20},{20,24},{24,28},{28,0},{1,5},{5... | collective-permute-start | bytes 294920 | tf_op jit(solution)/shard_map/ppermute | solution.py:20
  8.4 26.0 %slice-start.2 = ((s8[4718592]{0:T(1024)(128)(4,1)}), s8[524288]{0:T(1024)(128)(4,1)S(1)}, s32[]{:S(2)}) async-start(s8[4718592]{0:T(1024)(128)(4,1)} %bitcast.5), calls=%async_computation.2 | async-start | bytes 1048576
  14.8 19.6 %slice-start = ((s8[4718592]{0:T(1024)(128)(4,1)}), s8[4194304]{0:T(1024)(128)(4,1)S(1)}, s32[]{:S(2)}) async-start(s8[4718592]{0:T(1024)(128)(4,1)} %bitcast.3), calls=%async_computation | async-start | bytes 8388608
  15.7 18.7 %slice-start.1 = ((s8[4718592]{0:T(1024)(128)(4,1)}), s8[524288]{0:T(1024)(128)(4,1)S(1)}, s32[]{:S(2)}) async-start(s8[4718592]{0:T(1024)(128)(4,1)} %bitcast.3), calls=%async_computation.1 | async-start | bytes 1048576
  15.8 18.7 %slice-start.3 = ((s8[4718592]{0:T(1024)(128)(4,1)}), s8[4194304]{0:T(1024)(128)(4,1)S(1)}, s32[]{:S(2)}) async-start(s8[4718592]{0:T(1024)(128)(4,1)} %bitcast.5), calls=%async_computation.3 | async-start | bytes 8388608
  15.8 18.7 %copy-start = (bf16[4,24,1536]{2,1,0:T(8,128)(2,1)S(1)}, bf16[4,24,1536]{2,1,0:T(8,128)(2,1)}, u32[]{:S(2)}) copy-start(bf16[4,24,1536]{2,1,0:T(8,128)(2,1)} %corner_ref.1) | copy-start | bytes 884740
  15.8 18.7 %copy-start.1 = (f32[8,3072]{1,0:T(8,128)S(1)}, f32[8,3072]{1,0:T(8,128)}, u32[]{:S(2)}) copy-start(f32[8,3072]{1,0:T(8,128)} %rhs_ref.1) | copy-start | bytes 294916

commit v2 on v1

v2 whole, which is shorter than its diff:
```python
import functools

import jax
import jax.numpy as jnp
from jax import lax
from jax.experimental import pallas as pl
from jax.experimental.pallas import tpu as pltpu
from jax.sharding import PartitionSpec as P

ITERS = 4
LANES = 128
WIDE = 256
SHIFT = 8
CHUNK = 512
HIGH = lax.Precision.HIGHEST
MESH = pl.DeviceIdType.MESH
NT = (((1,), (1,)), ((), ()))


def iterate_kernel(
    n_sub, rhs_ref, dual_hbm, precond_hbm, corner_ref, block_corner_ref, table_ref,
    part_ref, first_ref, second_ref,
    lam_out, res_out,
    dual_ref, precond_ref, D, R, L, V, prev_ref, first_prev, second_next, parts_ref, kinv_ref,
    Q1, Q2, QO, OH1, OH2, OHT,
    rx, dtx, drx, ltx, lrx, msem, psem, qsem, ssem, rsem, dssem, drsem, lssem, lrsem,
):
    j = lax.axis_index("sub")
    c = lax.axis_index("coarse")
    subs, br, order = dual_ref.shape
    bw = subs * br
    half = 2 * bw
    brows = bw // WIDE * 8
    kr = part_ref.shape[0]
    right = lax.rem(j + 1, n_sub)
    left = lax.rem(j + n_sub - 1, n_sub)
    high = c // 2
    halo = lax.rem(j + 1 - 2 * high + n_sub, n_sub)
    halo_slot = 6 + c - 4 * high
    peers = [(j, lax.rem(c + o, 4)) for o in range(1, 4)]

    loads = [
        pltpu.make_async_copy(precond_hbm, precond_ref, msem.at[0]),
        pltpu.make_async_copy(dual_hbm, dual_ref, msem.at[1]),
    ]
    for copy in loads:
        copy.start()

    barrier = pltpu.get_barrier_semaphore()
    friends = list(peers)
    for o in range(4):
        friends += [(left, o), (right, o)]
    for o in range(2, n_sub - 1):
        friends.append((lax.rem(j + o, n_sub), c))
    for f in friends:
        pl.semaphore_signal(barrier, inc=1, device_id=f, device_id_type=MESH)
    pl.semaphore_wait(barrier, len(friends))

    setup = []
    plan = [
        (first_ref, first_prev, (right, c)),
        (second_ref, second_next, (left, c)),
        (rhs_ref, prev_ref, (right, c)),
    ] + [(part_ref, parts_ref.at[o], peers[o]) for o in range(3)]
    for i, (source, target, device) in enumerate(plan):
        copy = pltpu.make_async_remote_copy(
            src_ref=source, dst_ref=target, send_sem=psem.at[i], recv_sem=qsem.at[i],
            device_id=device, device_id_type=MESH,
        )
        copy.start()
        setup.append(copy)

    step_w = CHUNK
    chunks = half // step_w

    def chunk_at(o):
        return pl.ds(pl.multiple_of(o * step_w, step_w), step_w)

    def build(oh_ref, idx_ref):
        def body(o, carry):
            low = jnp.bitwise_and(idx_ref[:1, chunk_at(o)], WIDE - 1)
            rows = lax.broadcasted_iota(jnp.int32, (WIDE, step_w), 0)
            oh_ref[:, chunk_at(o)] = jnp.where(rows == low, 1.0, 0.0).astype(jnp.bfloat16)
            return carry

        lax.fori_loop(0, chunks, body, 0)

    def gather(src, idx_ref, oh_ref, finish, parts=1):
        count = src.shape[0] // 8 // parts

        def body(o, carry):
            hi = jnp.right_shift(idx_ref[:, chunk_at(o)], SHIFT)
            hi = jnp.broadcast_to(hi, (8, step_w))
            got = jnp.dot(src, oh_ref[:, chunk_at(o)], preferred_element_type=jnp.float32)
            acc = jnp.zeros((8, step_w), jnp.float32)
            for h in range(count):
                val = got[h * 8 : h * 8 + 8]
                for p in range(1, parts):
                    at = (p * count + h) * 8
                    val = val + got[at : at + 8]
                acc = jnp.where(hi == h, val, acc)
            finish(o, acc)
            return carry

        lax.fori_loop(0, chunks, body, 0)

    def put(ref, base):
        def finish(o, acc):
            ref[:, pl.ds(pl.multiple_of(base + o * step_w, step_w), step_w)] = acc

        return finish

    def put_index(ref):
        def finish(o, acc):
            pos = (acc[0:1] * WIDE + acc[1:2]).astype(jnp.int32)
            ref[:, chunk_at(o)] = jnp.broadcast_to(pos, (8, step_w))

        return finish

    def to_rows(x):
        return jnp.concatenate(
            [x[:, i * WIDE : (i + 1) * WIDE] for i in range(x.shape[1] // WIDE)], axis=0
        )

    def split(x):
        x = to_rows(x)
        a = x.astype(jnp.bfloat16)
        x = x - a.astype(jnp.float32)
        b = x.astype(jnp.bfloat16)
        x = x - b.astype(jnp.float32)
        return jnp.concatenate([a, b, x.astype(jnp.bfloat16)], axis=0)

    def inverse(idx_ref, shift, base, total):
        nh = half // WIDE
        acc = jnp.zeros((nh * 8, WIDE), jnp.float32)
        for o in range(chunks):
            rel = idx_ref[:, o * step_w : (o + 1) * step_w] + shift
            rel = jnp.where(rel < 0, rel + total, rel)
            hi = jnp.right_shift(rel, SHIFT)
            low = jnp.bitwise_and(rel, WIDE - 1)
            pos = lax.broadcasted_iota(jnp.int32, (nh * 8, step_w), 1) + (base + o * step_w)
            row = lax.broadcasted_iota(jnp.int32, (nh * 8, step_w), 0)
            digit = jnp.bitwise_and(row, 7)
            val = jnp.where(digit == 0, jnp.right_shift(pos, SHIFT), jnp.bitwise_and(pos, WIDE - 1))
            keep = jnp.logical_and(jnp.right_shift(row, 3) == hi, digit < 2)
            left_side = jnp.where(keep, val, 0).astype(jnp.float32).astype(jnp.bfloat16)
            rows = lax.broadcasted_iota(jnp.int32, (WIDE, step_w), 0)
            right_side = jnp.where(rows == low, 1.0, 0.0).astype(jnp.bfloat16)
            acc = acc + lax.dot_general(
                left_side, right_side, NT, preferred_element_type=jnp.float32
            )
        return acc

    total = n_sub * half
    pf_own = inverse(first_ref, -j * half, 0, total)
    ps = inverse(second_ref, -j * half, 0, total)
    for h in range(half // WIDE):
        pos = (pf_own[h * 8 : h * 8 + 1] * WIDE + pf_own[h * 8 + 1 : h * 8 + 2]).astype(jnp.int32)
        QO[:, h * WIDE : (h + 1) * WIDE] = jnp.broadcast_to(pos, (8, WIDE))
    Q1[...] = jnp.broadcast_to(first_ref[...] - j * half, (8, half))
    rel = second_ref[...] - j * half
    rel = jnp.where(rel < 0, rel + total, rel)
    rel = jnp.where(rel < half, rel, rel - (total - 2 * half))
    Q2[...] = jnp.broadcast_to(rel, (8, half))
    build(OH1, Q1)
    build(OH2, Q2)
    D[...] = jnp.zeros_like(D)
    L[...] = jnp.zeros_like(L)
    kinv_ref[...] = jnp.zeros_like(kinv_ref)
    parts_ref[3] = part_ref[...]
    own_rows = split(rhs_ref[...])
    gather(own_rows, Q1, OH1, put(R, 0), 3)
    for copy in setup:
        copy.wait_recv()
    for b in range(4):
        kinv_ref[b * kr : (b + 1) * kr] = parts_ref[lax.rem(c + 7 - b, 4)]
    prev_rows = split(prev_ref[...])
    n = half // WIDE * 8
    both = []
    for p in range(3):
        both += [own_rows[p * n : (p + 1) * n], prev_rows[p * n : (p + 1) * n]]
    gather(jnp.concatenate(both, axis=0), Q2, OH2, put(R, half), 3)
    ps = ps + inverse(second_next, -j * half, half, total)
    pf_prev = inverse(first_prev, -left * half, half, total)
    gather(ps.astype(jnp.bfloat16), Q1, OH1, put_index(Q1))
    pf = jnp.concatenate([pf_own, pf_prev], axis=0).astype(jnp.bfloat16)
    gather(pf, Q2, OH2, put_index(Q2))
    build(OH1, Q1)
    build(OH2, Q2)
    for copy in setup:
        copy.wait_send()

    def gathered(ref, s):
        parts = []
        for b in range(4):
            part = ref[:, b * bw + s * br : b * bw + (s + 1) * br]
            parts.append(part if b < 2 else -part)
        return jnp.concatenate(parts, axis=1).astype(jnp.bfloat16)

    def unpack(block):
        wide = block.astype(jnp.float32)
        return jnp.concatenate([wide[i * 8 : i * 8 + 8] for i in range(brows // 8)], axis=1)

    def exchange(app, terms, vec_ref):
        rx[app, 0] = to_rows(terms).astype(jnp.bfloat16)
        copies = []
        for i in range(7):
            if i < 4:
                slot, device = halo_slot, (halo, i)
            else:
                slot, device = i - 3, peers[i - 4]
            copy = pltpu.make_async_remote_copy(
                src_ref=rx.at[app, 0], dst_ref=rx.at[app, slot],
                send_sem=ssem.at[i], recv_sem=rsem.at[app, slot - 1],
                device_id=device, device_id_type=MESH,
            )
            copy.start()
            copies.append(copy)
        for slot in range(1, 4):
            pltpu.make_async_copy(
                rx.at[app, slot], rx.at[app, slot], rsem.at[app, slot - 1]
            ).wait()
        packed = [rx[app, lax.rem(c + 4 - b, 4)] for b in range(4)]
        blocks = [unpack(p) for p in packed]
        part = jnp.zeros((8, LANES), jnp.float32)
        for b in range(4):
            prod = vec_ref[:, b * bw : (b + 1) * bw] * blocks[b]
            for k in range(bw // LANES):
                piece = prod[:, k * LANES : (k + 1) * LANES]
                part = part + piece if b < 2 else part - piece
        dtx[app] = part
        dots = []
        for o in range(1, n_sub):
            copy = pltpu.make_async_remote_copy(
                src_ref=dtx.at[app], dst_ref=drx.at[app, o - 1],
                send_sem=dssem.at[o - 1], recv_sem=drsem.at[app],
                device_id=(lax.rem(j + o, n_sub), c), device_id_type=MESH,
            )
            copy.start()
            dots.append(copy)
        for b in range(4):
            V[:, b * bw : (b + 1) * bw] = blocks[b]
        for slot in range(4, 8):
            pltpu.make_async_copy(
                rx.at[app, slot], rx.at[app, slot], rsem.at[app, slot - 1]
            ).wait()

        def less(o, acc):
            V[:, chunk_at(o)] = V[:, chunk_at(o)] - acc

        def more(o, acc):
            at = pl.ds(pl.multiple_of(half + o * step_w, step_w), step_w)
            V[:, at] = acc - V[:, at]

        gather(
            jnp.concatenate([packed[2], packed[3], rx[app, 4], rx[app, 5]], axis=0),
            Q1, OH1, less,
        )
        gather(
            jnp.concatenate([packed[0], packed[1], rx[app, 6], rx[app, 7]], axis=0),
            Q2, OH2, more,
        )
        pltpu.make_async_copy(drx.at[app], drx.at[app], drsem.at[app]).wait()
        total = part
        for o in range(n_sub - 1):
            total = total + drx[app, o]
        for copy in copies + dots:
            copy.wait_send()
        return jnp.sum(total, axis=1, keepdims=True)

    def product(ops_ref, vecs):
        return [
            lax.dot_general(vecs[s], ops_ref[s], NT, preferred_element_type=jnp.float32)
            for s in range(subs)
        ]

    for copy in loads:
        copy.wait()

    def body(step, fit):
        vecs = [gathered(R, s) for s in range(subs)]
        terms = jnp.concatenate(product(precond_ref, vecs), axis=1)
        fit_next = exchange(2 * step, terms, R)
        D[...] = V[...] + (fit_next / fit) * D[...]

        vecs = [gathered(D, s) for s in range(subs)]
        load = jnp.zeros((8, kinv_ref.shape[0]), jnp.float32)
        for s in range(subs):
            lifted = lax.dot_general(
                vecs[s], corner_ref[s], NT, preferred_element_type=jnp.float32
            )
            load = load + jnp.dot(
                lifted, table_ref[s], precision=HIGH, preferred_element_type=jnp.float32
            )
        ltx[step] = load
        sent = []
        for o in range(1, n_sub):
            copy = pltpu.make_async_remote_copy(
                src_ref=ltx.at[step], dst_ref=lrx.at[step, o - 1],
                send_sem=lssem.at[o - 1], recv_sem=lrsem.at[step],
                device_id=(lax.rem(j + o, n_sub), c), device_id_type=MESH,
            )
            copy.start()
            sent.append(copy)
        outs = product(dual_ref, vecs)
        pltpu.make_async_copy(lrx.at[step], lrx.at[step], lrsem.at[step]).wait()
        for o in range(n_sub - 1):
            load = load + lrx[step, o]
        answer = lax.dot_general(
            load, kinv_ref[...], NT, precision=HIGH, preferred_element_type=jnp.float32
        ).astype(jnp.bfloat16)
        wide = answer.astype(jnp.float32)
        for s in range(subs):
            spread = lax.dot_general(
                wide, table_ref[s], NT, preferred_element_type=jnp.float32
            ).astype(jnp.bfloat16)
            outs[s] = outs[s] + jnp.dot(
                spread, block_corner_ref[s], preferred_element_type=jnp.float32
            )
        energy = exchange(2 * step + 1, jnp.concatenate(outs, axis=1), D)
        for copy in sent:
            copy.wait_send()
        alpha = fit_next / energy
        L[...] = L[...] + alpha * D[:, :half]
        R[...] = R[...] - alpha * V[...]
        return fit_next

    lax.fori_loop(0, ITERS, body, jnp.ones((8, 1), jnp.float32))
    build(OHT, QO)
    gather(split(L[...]), QO, OHT, put(lam_out, 0), 3)
    gather(split(R[:, :half]), QO, OHT, put(res_out, 0), 3)


def per_device(
    right_side, dual_ops, precond_ops, corner_ops, coarse_inverse, sub_index, corner_map
):
    cases, lam = right_side.shape
    subs, br, order = dual_ops.shape
    kr, ncg = coarse_inverse.shape
    n_sub = lax.axis_size("sub")
    mine = lax.axis_index("coarse")
    slots = sub_index.reshape(subs, 4, br).transpose(1, 0, 2).reshape(2, 1, lam)
    pad = -ncg % LANES
    part = jnp.pad(coarse_inverse, ((0, 0), (0, pad)))
    table = (corner_map[:, :, None] == jnp.arange(ncg + pad)[None, None, :]).astype(jnp.float32)
    block_corner = lax.dynamic_slice_in_dim(corner_ops, mine * br, br, 2)
    bw = subs * br
    vmem = pl.BlockSpec(memory_space=pltpu.VMEM)
    hbm = pl.BlockSpec(memory_space=pl.ANY)
    f32 = lambda *dims: pltpu.VMEM(dims, jnp.float32)
    i32 = lambda *dims: pltpu.VMEM(dims, jnp.int32)
    b16 = lambda *dims: pltpu.VMEM(dims, jnp.bfloat16)
    dma = pltpu.SemaphoreType.DMA
    out = jax.ShapeDtypeStruct((cases, lam), jnp.float32)
    return pl.pallas_call(
        functools.partial(iterate_kernel, n_sub),
        out_shape=[out, out],
        in_specs=[vmem, hbm, hbm] + [vmem] * 6,
        out_specs=[vmem] * 2,
        scratch_shapes=[
            b16(subs, br, order), b16(subs, br, order),
            f32(8, 2 * lam), f32(8, 2 * lam), f32(8, lam), f32(8, 2 * lam), f32(8, lam),
            i32(1, lam), i32(1, lam), f32(4, kr, ncg + pad), f32(ncg + pad, ncg + pad),
            i32(8, lam), i32(8, lam), i32(8, lam),
            b16(WIDE, lam), b16(WIDE, lam), b16(WIDE, lam),
            b16(2 * ITERS, 8, bw // WIDE * 8, WIDE),
            f32(2 * ITERS, 8, LANES), f32(2 * ITERS, n_sub - 1, 8, LANES),
            f32(ITERS, 8, ncg + pad), f32(ITERS, n_sub - 1, 8, ncg + pad),
            dma((2,)), dma((6,)), dma((6,)),
            dma((7,)), dma((2 * ITERS, 7)),
            dma((n_sub - 1,)), dma((2 * ITERS,)),
            dma((n_sub - 1,)), dma((ITERS,)),
        ],
        compiler_params=pltpu.CompilerParams(
            collective_id=0, has_side_effects=True, vmem_limit_bytes=48 * 2**20
        ),
        name="iterate",
    )(
        right_side, dual_ops, precond_ops, corner_ops, block_corner, table,
        part, slots[0], slots[1],
    )


def solution(mesh):
    placed = (
        P(None, "sub"),
        P("sub", "coarse", None),
        P("sub", "coarse", None),
        P("sub", None, None),
        P("coarse", None),
        P("sub", None),
        P("sub", None),
    )
    return jax.shard_map(
        per_device,
        mesh=mesh,
        in_specs=placed,
        out_specs=(P(None, "sub"), P(None, "sub")),
        check_vma=False,
    )
```

time: 174 us -> 125 us (0.72)
  Pallas kernels: 156 us -> 115 us
  starting transfers between devices: 6.12 us -> 0 us
  blocking collectives: 5.41 us -> 0 us
  local copies, waits for them, and re-layouts: 4.81 us -> 7.84 us
    pallas_call x1, Pallas kernels: 138 us -> 115 us  [per_device(): pl.pallas_call(functools.partial(iterate_kernel, n_sub), out_shape=[out,...]
    pallas_call x1 -> x0, Pallas kernels: 17.7 us -> none  [per_device(): pl.pallas_call(search_kernel, out_shape=[index] * 3, in_specs=[vmem] * 5,...]
    ppermute x3 -> x0, starting transfers between devices: 6.12 us -> none  [passed_along(): return lax.ppermute(value, axis, pairs)]
    all_gather x1 -> x0, blocking collectives: 5.41 us -> none  [per_device(): kinv = lax.all_gather(coarse_inverse, 'coarse', axis=0, tiled=True)]
    unnamed x14 -> x8, local copies, waits for them, and re-layouts: 1.32 us -> 5.47 us
    broadcast_in_dim x5 -> x0, local copies, waits for them, and re-layouts: 1.78 us -> none  [the longest x2 1.73 us: per_device(): wide = lambda x: jnp.broadcast_to(x[:, None], (x.shape[0], LANES))]
  transfers between devices with their start and end apart: 3 -> 0, of which waited for: 0 -> 0; matrix products, arithmetic and copies ran while one was open for 2% -> 0% of each run, Pallas kernels for 10% -> 0%
where the time goes in v2:
time: 125 us; the launch traced here: 124 us
  Pallas kernels  115 us (92%)
  local copies, waits for them, and re-layouts  7.84 us (6%)
    pallas_call x1, Pallas kernels, per_device(): pl.pallas_call(functools.partial(iterate_kernel, n_sub), out_shape=[out,...  115 us
    unnamed x8, local copies, waits for them, and re-layouts  5.47 us

profile of v2, /device:TPU:0, one launch (start us, length us, event | category | flops | bytes accessed | tf_op | source)
XLA Modules:
  0.0 124.3 jit_solution(13803533769977957800)
XLA Ops:
  0.6 0.7 pad.4.part_ref
  1.3 0.7 fusion.1
  2.1 0.8 fusion.table_ref
  2.9 0.9 constant_dynamic-slice_fusion.block_corner_ref
  3.8 0.0 copy-start
  3.8 2.3 %copy-done = bf16[4,384,1536]{2,1,0:T(8,128)(2,1)S(1)} copy-done((bf16[4,384,1536]{2,1,0:T(8,128)(2,1)S(1)}, bf16[4,384,1536]{2,1,0:T(8,128)(2,1)}, u32[]{:S(2)}) %copy-start) | copy-done | bytes 4718616
  6.1 0.0 copy-start.1
  6.1 1.0 copy-done.1
  7.1 0.0 copy-start.2
  7.1 0.9 copy-done.2
  8.0 115.0 %iterate.1 = (f32[8,3072]{1,0:T(8,128)S(1)}, f32[8,3072]{1,0:T(8,128)S(1)}) custom-call(f32[8,3072]{1,0:T(8,128)S(1)} %copy-done.2, bf16[4,384,1536]{2,1,0:T(8,128)(2,1)S(1)} %copy-done, bf16[4,384,1536]{2,1,0:T(8,128)(2,1)} %precond_hbm.1, bf16[4,24,1536]{2,1,0:T(8,128)(2,1)S(1)} %copy-done.1, ...), custom_call_target="tpu_custom_call" | custom-call | tf_op jit(solution)/shard_map/iterate/pallas_call | solution.py:355
  123.0 0.6 copy.12
  123.7 0.6 copy.13
  (2 shorter events, 0.0 us)
Async XLA Ops:
  3.8 2.3 %copy-start = (bf16[4,384,1536]{2,1,0:T(8,128)(2,1)S(1)}, bf16[4,384,1536]{2,1,0:T(8,128)(2,1)}, u32[]{:S(2)}) copy-start(bf16[4,384,1536]{2,1,0:T(8,128)(2,1)} %dual_hbm.1) | copy-start | bytes 14155780
  6.1 1.0 copy-start.1
  7.1 0.9 copy-start.2

commit v3 on v2

--- a/solution.py
+++ b/solution.py
@@ -18,9 +18,9 @@
 
 
 def iterate_kernel(
-    n_sub, rhs_ref, dual_hbm, precond_hbm, corner_ref, block_corner_ref, table_ref,
-    part_ref, first_ref, second_ref,
+    n_sub, rhs_hbm, dual_hbm, precond_hbm, corner_hbm, inverse_hbm, index_hbm, map_hbm,
     lam_out, res_out,
+    rhs_ref, corner_ref, part_ref, index_ref, map_ref, first_ref, second_ref, CT, CB, load_ref,
     dual_ref, precond_ref, D, R, L, V, prev_ref, first_prev, second_next, parts_ref, kinv_ref,
     Q1, Q2, QO, OH1, OH2, OHT,
     rx, dtx, drx, ltx, lrx, msem, psem, qsem, ssem, rsem, dssem, drsem, lssem, lrsem,
@@ -39,6 +39,15 @@
     halo_slot = 6 + c - 4 * high
     peers = [(j, lax.rem(c + o, 4)) for o in range(1, 4)]
 
+    smalls = [
+        (index_hbm, index_ref), (rhs_hbm, rhs_ref), (inverse_hbm, part_ref),
+        (map_hbm, map_ref), (corner_hbm, corner_ref),
+    ]
+    smalls = [
+        pltpu.make_async_copy(a, b, msem.at[2 + i]) for i, (a, b) in enumerate(smalls)
+    ]
+    for copy in smalls:
+        copy.start()
     loads = [
         pltpu.make_async_copy(precond_hbm, precond_ref, msem.at[0]),
         pltpu.make_async_copy(dual_hbm, dual_ref, msem.at[1]),
@@ -54,6 +63,13 @@
         friends.append((lax.rem(j + o, n_sub), c))
     for f in friends:
         pl.semaphore_signal(barrier, inc=1, device_id=f, device_id_type=MESH)
+    for copy in smalls:
+        copy.wait()
+    for b in range(4):
+        ref = first_ref if b < 2 else second_ref
+        for s in range(subs):
+            at = (b % 2) * bw + s * br
+            ref[:, at : at + br] = index_ref[s : s + 1, b * br : (b + 1) * br]
     pl.semaphore_wait(barrier, len(friends))
 
     setup = []
@@ -167,13 +183,22 @@
     D[...] = jnp.zeros_like(D)
     L[...] = jnp.zeros_like(L)
     kinv_ref[...] = jnp.zeros_like(kinv_ref)
+    load_ref[...] = jnp.zeros_like(load_ref)
+    for s in range(subs):
+        rows = lax.broadcasted_iota(jnp.int32, (CT.shape[1], map_ref.shape[1]), 0)
+        table = jnp.where(rows == map_ref[s : s + 1, :], 1.0, 0.0).astype(jnp.bfloat16)
+        CT[s] = jnp.dot(
+            table, corner_ref[s], preferred_element_type=jnp.float32
+        ).astype(jnp.bfloat16)
+        at = pl.ds(pl.multiple_of(c * br, br), br)
+        CB[:, s * br : (s + 1) * br] = CT[s, :, at]
     parts_ref[3] = part_ref[...]
     own_rows = split(rhs_ref[...])
     gather(own_rows, Q1, OH1, put(R, 0), 3)
     for copy in setup:
         copy.wait_recv()
     for b in range(4):
-        kinv_ref[b * kr : (b + 1) * kr] = parts_ref[lax.rem(c + 7 - b, 4)]
+        kinv_ref[b * kr : (b + 1) * kr, : part_ref.shape[1]] = parts_ref[lax.rem(c + 7 - b, 4)]
     prev_rows = split(prev_ref[...])
     n = half // WIDE * 8
     both = []
@@ -260,6 +285,9 @@
             jnp.concatenate([packed[0], packed[1], rx[app, 6], rx[app, 7]], axis=0),
             Q2, OH2, more,
         )
+        return part, copies, dots
+
+    def finish_dot(app, part, copies, dots):
         pltpu.make_async_copy(drx.at[app], drx.at[app], drsem.at[app]).wait()
         total = part
         for o in range(n_sub - 1):
@@ -280,17 +308,12 @@
     def body(step, fit):
         vecs = [gathered(R, s) for s in range(subs)]
         terms = jnp.concatenate(product(precond_ref, vecs), axis=1)
-        fit_next = exchange(2 * step, terms, R)
-        D[...] = V[...] + (fit_next / fit) * D[...]
-
-        vecs = [gathered(D, s) for s in range(subs)]
+        pending = exchange(2 * step, terms, R)
+
         load = jnp.zeros((8, kinv_ref.shape[0]), jnp.float32)
         for s in range(subs):
-            lifted = lax.dot_general(
-                vecs[s], corner_ref[s], NT, preferred_element_type=jnp.float32
-            )
-            load = load + jnp.dot(
-                lifted, table_ref[s], precision=HIGH, preferred_element_type=jnp.float32
+            load = load + lax.dot_general(
+                gathered(V, s), CT[s], NT, preferred_element_type=jnp.float32
             )
         ltx[step] = load
         sent = []
@@ -302,22 +325,22 @@
             )
             copy.start()
             sent.append(copy)
-        outs = product(dual_ref, vecs)
+        fit_next = finish_dot(2 * step, *pending)
+        beta = fit_next / fit
+        D[...] = V[...] + beta * D[...]
+
+        vecs = [gathered(D, s) for s in range(subs)]
+        terms = jnp.concatenate(product(dual_ref, vecs), axis=1)
         pltpu.make_async_copy(lrx.at[step], lrx.at[step], lrsem.at[step]).wait()
         for o in range(n_sub - 1):
             load = load + lrx[step, o]
+        load = load + beta * load_ref[...]
+        load_ref[...] = load
         answer = lax.dot_general(
             load, kinv_ref[...], NT, precision=HIGH, preferred_element_type=jnp.float32
         ).astype(jnp.bfloat16)
-        wide = answer.astype(jnp.float32)
-        for s in range(subs):
-            spread = lax.dot_general(
-                wide, table_ref[s], NT, preferred_element_type=jnp.float32
-            ).astype(jnp.bfloat16)
-            outs[s] = outs[s] + jnp.dot(
-                spread, block_corner_ref[s], preferred_element_type=jnp.float32
-            )
-        energy = exchange(2 * step + 1, jnp.concatenate(outs, axis=1), D)
+        terms = terms + jnp.dot(answer, CB[...], preferred_element_type=jnp.float32)
+        energy = finish_dot(2 * step + 1, *exchange(2 * step + 1, terms, D))
         for copy in sent:
             copy.wait_send()
         alpha = fit_next / energy
@@ -338,12 +361,8 @@
     subs, br, order = dual_ops.shape
     kr, ncg = coarse_inverse.shape
     n_sub = lax.axis_size("sub")
-    mine = lax.axis_index("coarse")
-    slots = sub_index.reshape(subs, 4, br).transpose(1, 0, 2).reshape(2, 1, lam)
     pad = -ncg % LANES
-    part = jnp.pad(coarse_inverse, ((0, 0), (0, pad)))
-    table = (corner_map[:, :, None] == jnp.arange(ncg + pad)[None, None, :]).astype(jnp.float32)
-    block_corner = lax.dynamic_slice_in_dim(corner_ops, mine * br, br, 2)
+    nc = corner_map.shape[1]
     bw = subs * br
     vmem = pl.BlockSpec(memory_space=pltpu.VMEM)
     hbm = pl.BlockSpec(memory_space=pl.ANY)
@@ -355,18 +374,21 @@
     return pl.pallas_call(
         functools.partial(iterate_kernel, n_sub),
         out_shape=[out, out],
-        in_specs=[vmem, hbm, hbm] + [vmem] * 6,
+        in_specs=[hbm] * 7,
         out_specs=[vmem] * 2,
         scratch_shapes=[
+            f32(8, lam), b16(subs, nc, order), f32(kr, ncg), i32(subs, order), i32(subs, nc),
+            i32(1, lam), i32(1, lam), b16(subs, ncg + pad, order), b16(ncg + pad, bw),
+            f32(8, ncg + pad),
             b16(subs, br, order), b16(subs, br, order),
             f32(8, 2 * lam), f32(8, 2 * lam), f32(8, lam), f32(8, 2 * lam), f32(8, lam),
-            i32(1, lam), i32(1, lam), f32(4, kr, ncg + pad), f32(ncg + pad, ncg + pad),
+            i32(1, lam), i32(1, lam), f32(4, kr, ncg), f32(ncg + pad, ncg + pad),
             i32(8, lam), i32(8, lam), i32(8, lam),
             b16(WIDE, lam), b16(WIDE, lam), b16(WIDE, lam),
             b16(2 * ITERS, 8, bw // WIDE * 8, WIDE),
             f32(2 * ITERS, 8, LANES), f32(2 * ITERS, n_sub - 1, 8, LANES),
             f32(ITERS, 8, ncg + pad), f32(ITERS, n_sub - 1, 8, ncg + pad),
-            dma((2,)), dma((6,)), dma((6,)),
+            dma((7,)), dma((6,)), dma((6,)),
             dma((7,)), dma((2 * ITERS, 7)),
             dma((n_sub - 1,)), dma((2 * ITERS,)),
             dma((n_sub - 1,)), dma((ITERS,)),
@@ -376,8 +398,7 @@
         ),
         name="iterate",
     )(
-        right_side, dual_ops, precond_ops, corner_ops, block_corner, table,
-        part, slots[0], slots[1],
+        right_side, dual_ops, precond_ops, corner_ops, coarse_inverse, sub_index, corner_map,
     )
 
 

time: 125 us -> 119 us (0.952)
  Pallas kernels: 115 us -> 110 us
    pallas_call x1, Pallas kernels: 115 us -> 110 us  [per_device(): pl.pallas_call(functools.partial(iterate_kernel, n_sub), out_shape=[out,...]
    unnamed x8 -> x14, local copies, waits for them, and re-layouts: 5.47 us -> 7.58 us
where the time goes in v3:
time: 119 us
  Pallas kernels  110 us (92%)
  local copies, waits for them, and re-layouts  7.58 us (6%)
    pallas_call x1, Pallas kernels, per_device(): pl.pallas_call(functools.partial(iterate_kernel, n_sub), out_shape=[out,...  110 us
    unnamed x14, local copies, waits for them, and re-layouts  7.58 us

profile of v3, /device:TPU:0, one launch (start us, length us, event | category | flops | bytes accessed | tf_op | source)
XLA Modules:
  0.0 118.6 jit_solution(4951219001872930768)
XLA Ops:
  0.6 0.0 copy-start
  0.6 2.3 %copy-done = bf16[4,384,1536]{2,1,0:T(8,128)(2,1)S(1)} copy-done((bf16[4,384,1536]{2,1,0:T(8,128)(2,1)S(1)}, bf16[4,384,1536]{2,1,0:T(8,128)(2,1)}, u32[]{:S(2)}) %copy-start) | copy-done | bytes 4718616
  3.0 0.0 copy-start.1
  3.0 1.0 copy-done.1
  3.9 0.0 copy-start.2
  3.9 0.9 copy-done.2
  4.8 0.0 copy-start.3
  4.8 0.7 copy-done.3
  5.6 0.0 copy-start.4
  5.6 0.7 copy-done.4
  6.3 0.0 copy-start.5
  6.3 0.7 copy-done.5
  6.9 110.3 %iterate.1 = (f32[8,3072]{1,0:T(8,128)S(1)}, f32[8,3072]{1,0:T(8,128)S(1)}) custom-call(f32[8,3072]{1,0:T(8,128)S(1)} %copy-done.2, bf16[4,384,1536]{2,1,0:T(8,128)(2,1)S(1)} %copy-done, bf16[4,384,1536]{2,1,0:T(8,128)(2,1)} %precond_hbm.1, bf16[4,24,1536]{2,1,0:T(8,128)(2,1)S(1)} %copy-done.1, f32[16,64]{1,0:T(8,128)S(1)} %copy-done.4, ...), custom_call_target="tpu_custom_call" | custom-call | tf_op jit(solution)/shard_map/iterate/pallas_call | solution.py:374
  117.3 0.6 copy.11
  117.9 0.6 copy.12
Async XLA Ops:
  0.6 2.3 %copy-start = (bf16[4,384,1536]{2,1,0:T(8,128)(2,1)S(1)}, bf16[4,384,1536]{2,1,0:T(8,128)(2,1)}, u32[]{:S(2)}) copy-start(bf16[4,384,1536]{2,1,0:T(8,128)(2,1)} %dual_hbm.1) | copy-start | bytes 14155780
  3.0 1.0 copy-start.1
  3.9 0.9 copy-start.2
  4.8 0.7 copy-start.3
  5.6 0.7 copy-start.4
  6.3 0.7 copy-start.5

commit v4 on v3

--- a/solution.py
+++ b/solution.py
@@ -118,7 +118,7 @@
             finish(o, acc)
             return carry
 
-        lax.fori_loop(0, chunks, body, 0)
+        lax.fori_loop(0, chunks, body, 0, unroll=True)
 
     def put(ref, base):
         def finish(o, acc):
@@ -365,7 +365,7 @@
     nc = corner_map.shape[1]
     bw = subs * br
     vmem = pl.BlockSpec(memory_space=pltpu.VMEM)
-    hbm = pl.BlockSpec(memory_space=pl.ANY)
+    hbm = pl.BlockSpec(memory_space=pltpu.HBM)
     f32 = lambda *dims: pltpu.VMEM(dims, jnp.float32)
     i32 = lambda *dims: pltpu.VMEM(dims, jnp.int32)
     b16 = lambda *dims: pltpu.VMEM(dims, jnp.bfloat16)

time: 119 us -> 104 us (0.87)
  Pallas kernels: 110 us -> 95.4 us
    pallas_call x1, Pallas kernels: 110 us -> 95.4 us  [per_device(): pl.pallas_call(functools.partial(iterate_kernel, n_sub), out_shape=[out,...]
where the time goes in v4:
time: 104 us
  Pallas kernels  95.4 us (92%)
  local copies, waits for them, and re-layouts  7.58 us (7%)
    pallas_call x1, Pallas kernels, per_device(): pl.pallas_call(functools.partial(iterate_kernel, n_sub), out_shape=[out,...  95.4 us
    unnamed x14, local copies, waits for them, and re-layouts  7.58 us

profile of v4, /device:TPU:0, one launch (start us, length us, event | category | flops | bytes accessed | tf_op | source)
XLA Modules:
  0.0 103.6 jit_solution(774405779569875803)
XLA Ops:
  0.6 0.0 copy-start
  0.6 2.3 %copy-done = bf16[4,384,1536]{2,1,0:T(8,128)(2,1)S(1)} copy-done((bf16[4,384,1536]{2,1,0:T(8,128)(2,1)S(1)}, bf16[4,384,1536]{2,1,0:T(8,128)(2,1)}, u32[]{:S(2)}) %copy-start) | copy-done | bytes 4718616
  3.0 0.0 copy-start.1
  3.0 1.0 copy-done.1
  3.9 0.0 copy-start.2
  3.9 0.9 copy-done.2
  4.8 0.0 copy-start.3
  4.8 0.7 copy-done.3
  5.6 0.0 copy-start.4
  5.6 0.7 copy-done.4
  6.3 0.0 copy-start.5
  6.3 0.7 copy-done.5
  6.9 95.4 %iterate.1 = (f32[8,3072]{1,0:T(8,128)S(1)}, f32[8,3072]{1,0:T(8,128)S(1)}) custom-call(f32[8,3072]{1,0:T(8,128)S(1)} %copy-done.2, bf16[4,384,1536]{2,1,0:T(8,128)(2,1)S(1)} %copy-done, bf16[4,384,1536]{2,1,0:T(8,128)(2,1)} %precond_hbm.1, bf16[4,24,1536]{2,1,0:T(8,128)(2,1)S(1)} %copy-done.1, f32[16,64]{1,0:T(8,128)S(1)} %copy-done.4, ...), custom_call_target="tpu_custom_call" | custom-call | tf_op jit(solution)/shard_map/iterate/pallas_call | solution.py:374
  102.4 0.6 copy.11
  103.0 0.6 copy.12
Async XLA Ops:
  0.6 2.3 %copy-start = (bf16[4,384,1536]{2,1,0:T(8,128)(2,1)S(1)}, bf16[4,384,1536]{2,1,0:T(8,128)(2,1)}, u32[]{:S(2)}) copy-start(bf16[4,384,1536]{2,1,0:T(8,128)(2,1)} %dual_hbm.1) | copy-start | bytes 14155780
  3.0 1.0 copy-start.1
  3.9 0.9 copy-start.2
  4.8 0.7 copy-start.3
  5.6 0.7 copy-start.4
  6.3 0.7 copy-start.5
